TPU v7x, 256 devices: a whole 4x4x8 slice. The times are simulated.
256 devices in a mesh: tm: 32 (over y, z), head: 4 (over x_hi, core), dp: 2 (over x_lo).
Axes of the slice: x: 4 (x_hi: 2, x_lo: 2; x = x_hi * 2 + x_lo), y: 4, z: 8, core: 2. Of those that a mesh axis runs over, the one named last changes fastest.
Arguments:
- qkv: bfloat16 [2, 24576, 3, 1536], P('dp', ('tm', 'head')), may hold values from -6 to 6
- norm_gains: float32 [2, 128], replicated, may hold values from 0.1 to 1.9
- windows: int32 [12, 2], P('head'), may hold values from 0 to 1, as said below
- proj_weight: bfloat16 [1536, 3072], P(('head', 'dp')), may hold values from -0.15625 to 0.15625
- target: bfloat16 [2, 24576, 3072], P('dp', ('tm', 'head')), may hold values from -0.3125 to 0.3125
- stream_ids: int32 [2, 24576], P('dp', ('tm', 'head')), may hold values from 0 to 3
- ema_value: float32 [4], replicated, may hold values from 0.3 to 3
- ema_steps: int32 [4], replicated, may hold values from 1 to 299
Outputs:
- grad_qkv: bfloat16 [2, 24576, 3, 1536], P('dp', ('tm', 'head'))
- grad_proj: float32 [1536, 3072], P(('head', 'dp'))
- grad_gains: float32 [2, 128], replicated
Inputs may be any that keep to these rules, and one draw needn't show every extreme that they name: `windows`: every entry is 0 or 1, and some head has 1 in both columns.
All inputs are finite; a program needn't handle non-finite values.
Results may differ from a plain program's by a relative error of at most 0.015.
The roundings to bfloat16 on the way count: a program that leaves them out, or rounds other values in their place, can miss the bound.
Values may be sent and summed in bfloat16 or wider, within the bound.
A program may use at most 192 MiB of HBM per device.

v0:
```python
import jax
import jax.numpy as jnp
from jax import lax
from jax.sharding import PartitionSpec as P

TILE = 384


EPSILON = 1e-06
DECAY_RATE = 0.99


def with_halo(cells, sides, width):
    for axis, dim in sides:
        count = lax.axis_size(axis)
        ends = count - 1
        head = lax.slice_in_dim(cells, 0, width, axis=dim)
        tail = lax.slice_in_dim(cells, cells.shape[dim] - width, cells.shape[dim], axis=dim)
        cells = jnp.concatenate(
            [
                lax.ppermute(tail, axis, [(i, (i + 1) % count) for i in range(ends)]),
                cells,
                lax.ppermute(head, axis, [((i + 1) % count, i) for i in range(ends)]),
            ],
            axis=dim,
        )
    return cells


def shifted(array, axis, by):
    devices = lax.axis_size(axis)
    pairs = [(i, i + by) for i in range(devices) if 0 <= i + by < devices]
    return lax.ppermute(array, axis, pairs)


def norm_forward(raw_part, gain_row):
    widened = raw_part.astype(jnp.float32)
    inverse = lax.rsqrt(jnp.mean(widened * widened, axis=-1, keepdims=True) + EPSILON)
    normed = widened * inverse
    return ((normed * gain_row).astype(jnp.bfloat16), normed, inverse)


def norm_backward(grad_normed, normed, inverse, gain_row):
    grad_unit = grad_normed * gain_row
    grad_input = inverse * (
        grad_unit - normed * jnp.mean(grad_unit * normed, axis=-1, keepdims=True)
    )
    grad_gain = jnp.sum((grad_normed * normed).reshape(-1, normed.shape[-1]), axis=0)
    return (grad_input, grad_gain)


def tile_allowed(reach, slab_len, slab_pos, slab_count):
    query_pos = jnp.arange(slab_len, dtype=jnp.int32)
    key_pos = jnp.arange(3 * slab_len, dtype=jnp.int32)
    offset = key_pos // slab_len - 1
    present = (slab_pos + offset >= 0) & (slab_pos + offset < slab_count)
    tile_gap = jnp.abs(query_pos[:, None] // TILE - key_pos[None, :] % slab_len // TILE)
    return present[None, :] & (jnp.abs(offset)[None, :] <= reach[0]) & (tile_gap <= reach[1])


def contract(left_arr, right_arr, left_dim, right_dim):
    return lax.dot_general(
        left_arr,
        right_arr,
        (((left_dim,), (right_dim,)), ((), ())),
        preferred_element_type=jnp.float32,
    )


def per_device(qkv, norm_gains, windows, proj_weight, target, stream_ids, ema_value, ema_steps):
    in_heads = lax.all_to_all(qkv, "head", split_axis=3, concat_axis=1, tiled=True)
    slab_len = in_heads.shape[1]
    heads_here = windows.shape[0]
    head_dim = norm_gains.shape[1]
    width_here = heads_here * head_dim
    slab_pos = lax.axis_index("tm")
    slab_count = lax.axis_size("tm")
    score_scale = head_dim ** (-0.5)
    pieces = in_heads[0].reshape(slab_len, 3, heads_here, head_dim)
    queries, query_unit, query_inv = norm_forward(pieces[:, 0], norm_gains[0])
    keys_n, key_unit, key_inv = norm_forward(pieces[:, 1], norm_gains[1])
    values = pieces[:, 2]
    paired = jnp.stack([keys_n, values], axis=1).reshape(slab_len, 2, width_here)
    extended = with_halo(paired, (("tm", 0),), slab_len)
    extended = extended.reshape(3 * slab_len, 2, heads_here, head_dim)
    query_heads = queries.transpose(1, 0, 2)
    key_heads = extended[:, 0].transpose(1, 0, 2)
    value_heads = extended[:, 1].transpose(1, 0, 2)

    def attend(members):
        query_one, key_one, value_one, reach = members
        scores = contract(query_one, key_one, 1, 1) * score_scale
        allowed = tile_allowed(reach, slab_len, slab_pos, slab_count)
        raised = jnp.where(allowed, jnp.exp(scores), 0.0)
        chance_one = (raised / jnp.sum(raised, axis=-1, keepdims=True)).astype(jnp.bfloat16)
        mixed = jnp.dot(chance_one, value_one, preferred_element_type=jnp.float32).astype(
            jnp.bfloat16
        )
        return (mixed, chance_one)

    attended, chances = lax.map(attend, (query_heads, key_heads, value_heads, windows))
    attn_rows = attended.transpose(1, 0, 2).reshape(slab_len, width_here)
    proj_local = lax.all_gather(proj_weight, "dp", axis=0, tiled=True)
    outputs = lax.psum_scatter(
        jnp.dot(attn_rows, proj_local, preferred_element_type=jnp.float32).astype(jnp.bfloat16),
        "head",
        scatter_dimension=0,
        tiled=True,
    ).astype(jnp.float32)
    stream_count = ema_value.shape[0]
    corrected = ema_value / (1.0 - jnp.power(DECAY_RATE, ema_steps.astype(jnp.float32)))
    member = (stream_ids[0][:, None] == jnp.arange(stream_count, dtype=jnp.int32)[None, :]).astype(
        jnp.float32
    )
    token_weight = jnp.dot(member, 1.0 / corrected, precision=lax.Precision.HIGHEST)
    grad_rows = (token_weight[:, None] * (outputs - target[0].astype(jnp.float32))).astype(
        jnp.bfloat16
    )
    grad_slab = lax.all_gather(grad_rows, "head", axis=0, tiled=True)
    grad_attn = contract(grad_slab, proj_local, 1, 1).astype(jnp.bfloat16)
    grad_proj_local = contract(attn_rows, grad_slab, 0, 0)
    grad_heads = grad_attn.reshape(slab_len, heads_here, head_dim).transpose(1, 0, 2)

    def backprop(members):
        query_one, key_one, value_one, chance_one, grad_one = members
        grad_chances = contract(grad_one, value_one, 1, 1)
        spread = chance_one.astype(jnp.float32)
        diagonal = jnp.sum(spread * grad_chances, axis=-1, keepdims=True)
        grad_scores = (spread * (grad_chances - diagonal) * score_scale).astype(jnp.bfloat16)
        grad_query = jnp.dot(grad_scores, key_one, preferred_element_type=jnp.float32)
        grad_key = contract(grad_scores, query_one, 0, 0)
        grad_value = contract(chance_one, grad_one, 0, 0)
        return (grad_query, grad_key, grad_value)

    grad_query, grad_key, grad_value = lax.map(
        backprop, (query_heads, key_heads, value_heads, chances, grad_heads)
    )
    wide_grads = (
        jnp.stack([grad_key, grad_value], axis=0)
        .transpose(2, 0, 1, 3)
        .reshape(3 * slab_len, 2, width_here)
    )
    from_next = shifted(wide_grads[:slab_len].astype(jnp.bfloat16), "tm", -1).astype(jnp.float32)
    from_prev = shifted(wide_grads[2 * slab_len :].astype(jnp.bfloat16), "tm", 1).astype(
        jnp.float32
    )
    summed = wide_grads[slab_len : 2 * slab_len] + from_next + from_prev
    grad_keys_n = summed[:, 0].reshape(slab_len, heads_here, head_dim)
    grad_values = summed[:, 1].reshape(slab_len, heads_here, head_dim)
    grad_q_in, gain_query = norm_backward(
        grad_query.transpose(1, 0, 2), query_unit, query_inv, norm_gains[0]
    )
    grad_k_in, gain_key = norm_backward(grad_keys_n, key_unit, key_inv, norm_gains[1])
    grad_gains = lax.psum(jnp.stack([gain_query, gain_key], axis=0), ("tm", "head", "dp"))
    grad_local = (
        jnp.stack([grad_q_in, grad_k_in, grad_values], axis=1)
        .reshape(1, slab_len, 3, width_here)
        .astype(jnp.bfloat16)
    )
    grad_qkv = lax.all_to_all(grad_local, "head", split_axis=1, concat_axis=3, tiled=True)
    dp_count = lax.axis_size("dp")
    dp_rows = grad_proj_local.shape[0] // dp_count
    everything = lax.psum(grad_proj_local, ("tm", "dp"))
    grad_proj = lax.dynamic_slice_in_dim(everything, lax.axis_index("dp") * dp_rows, dp_rows, 0)
    return (grad_qkv, grad_proj, grad_gains)


def solution(mesh):
    return jax.shard_map(
        per_device,
        mesh=mesh,
        in_specs=(
            P("dp", ("tm", "head"), None, None),
            P(),
            P("head", None),
            P(("head", "dp"), None),
            P("dp", ("tm", "head"), None),
            P("dp", ("tm", "head")),
            P(),
            P(),
        ),
        out_specs=(P("dp", ("tm", "head"), None, None), P(("head", "dp"), None), P()),
        check_vma=False,
    )
```

profile of v0, /device:TPU:34, one launch (start us, length us, event | category | flops | bytes accessed | tf_op | source)
XLA Modules:
  0.0 991.9 jit_solution(16419751413891781272)
XLA Ops:
  7.2 5.5 copy.141
  12.7 3.8 all-to-all-start
  17.2 37.8 %all-to-all-done = bf16[1,192,3,1536]{1,2,0,3:T(4,128)(2,1)S(1)} async-done(((bf16[1,192,3,1536]{1,2,0,3:T(4,128)(2,1)}), bf16[1,192,3,1536]{1,2,0,3:T(4,128)(2,1)S(1)}, u32[]{:S(2)}, u32[]{:S(2)}) %all-to-all-start) | async-done | bytes 1769504 | tf_op jit(solution)/shard_map/all_to_all | solution.py:71
  58.2 4.6 reshape_squeeze.10
  74.7 3.8 collective-permute-start
  84.8 19.6 %collective-permute-done = bf16[768,2,384]{0,2,1:T(8,128)(2,1)} collective-permute-done((bf16[768,2,384]{0,2,1:T(8,128)(2,1)}, bf16[768,2,384]{0,2,1:T(8,128)(2,1)}, u32[]{:S(2)}, u32[]{:S(2)}) %collective-permute-start) | collective-permute-done | bytes 1179680 | tf_op jit(solution)/shard_map/ppermute | solution.py:21
  104.4 3.7 collective-permute-done.1
  116.4 35.8 %while.29 = (s32[]{:T(128)}, bf16[3,768,128]{1,2,0:T(8,128)(2,1)}, bf16[3,768,2304]{2,1,0:T(8,128)(2,1)}, s32[]{:T(128)}, s32[3,2]{0,1:T(2,128)S(1)}, /*index=5*...) while((s32[]{:T(128)}, bf16[3,768,128]{1,2,0:T(8,128)(2,1)}, ...), condition=%wide.region_4.5_spmd, body=%wide.region_2.4_spmd.sunk | while | flops 922067712 | bytes 27175304 | solution.py:101
  117.7 4.8 fusion.114
  129.6 4.8 fusion.114
  141.5 4.8 fusion.114
  152.2 7.3 convolution_convert_fusion.1
  160.4 59.0 %reduce-scatter.2.cloned.1.call-done = bf16[192,3072]{1,0:T(8,128)(2,1)} async-done(((bf16[768,3072]{1,0:T(8,128)(2,1)}), bf16[192,3072]{1,0:T(8,128)(2,1)}) %reduce-scatter.2.cloned.1.call-update) | async-done | bytes 1179664 | tf_op jit(solution)/shard_map/reduce_scatter | solution.py:104
  222.5 43.4 %all-gather.5.cloned.1.call-done = bf16[768,3072]{1,0:T(8,128)(2,1)} async-done(((bf16[192,3072]{1,0:T(8,128)(2,1)}), bf16[768,3072]{1,0:T(8,128)(2,1)}) %all-gather.5.cloned.1.call-update) | async-done | bytes 4718608 | tf_op jit(solution)/shard_map/all_gather | solution.py:119
  265.9 6.0 convolution_convert_fusion.2
  274.0 84.0 %while.30 = (s32[]{:T(128)}, f32[3,768,128]{2,0,1:T(4,128)}, f32[3,2304,128]{1,2,0:T(8,128)S(1)}, f32[3,2304,128]{1,2,0:T(8,128)}, bf16[3,768,2304]{2,1,0:T(8,12...) while((s32[]{:T(128)}, f32[3,768,128]{2,0,1:T(4,128)}, ...), condition=%wide.region_8.9_spmd, body=%wide.region_6.8_spmd.sunk | while | flops 1826094336 | bytes 69020336 | solution.py:135
  277.4 4.0 fusion.123
  286.9 11.1 %dynamic_update_slice.40 = f32[3,768,128]{2,0,1:T(4,128)} dynamic-update-slice(f32[3,768,128]{2,0,1:T(4,128)} %get-tuple-element.508, f32[1,768,128]{2,0,1:T(1,128)S(1)} %bitcast.200, s32[]{:T(128)} %get-tuple-element.507, s32[]{:T(128)} %constant.138.clone.1..sunk, s32[]{:T(128)} %constant.138.clone.1..sunk) | dynamic-update-slice | bytes 786436 | tf_op jit(solution)/shard_map/while/body/jit(dynamic_update_index_in_dim)/dynamic_update_slice | solution.py:135
  298.1 3.8 fusion.126
  305.4 4.0 fusion.123
  314.9 11.1 %dynamic_update_slice.40 = f32[3,768,128]{2,0,1:T(4,128)} dynamic-update-slice(f32[3,768,128]{2,0,1:T(4,128)} %get-tuple-element.508, f32[1,768,128]{2,0,1:T(1,128)S(1)} %bitcast.200, s32[]{:T(128)} %get-tuple-element.507, s32[]{:T(128)} %constant.138.clone.1..sunk, s32[]{:T(128)} %constant.138.clone.1..sunk) | dynamic-update-slice | bytes 786436 | tf_op jit(solution)/shard_map/while/body/jit(dynamic_update_index_in_dim)/dynamic_update_slice | solution.py:135
  326.1 3.8 fusion.126
  333.3 4.0 fusion.123
  342.9 11.1 %dynamic_update_slice.40 = f32[3,768,128]{2,0,1:T(4,128)} dynamic-update-slice(f32[3,768,128]{2,0,1:T(4,128)} %get-tuple-element.508, f32[1,768,128]{2,0,1:T(1,128)S(1)} %bitcast.200, s32[]{:T(128)} %get-tuple-element.507, s32[]{:T(128)} %constant.138.clone.1..sunk, s32[]{:T(128)} %constant.138.clone.1..sunk) | dynamic-update-slice | bytes 786436 | tf_op jit(solution)/shard_map/while/body/jit(dynamic_update_index_in_dim)/dynamic_update_slice | solution.py:135
  354.1 3.8 fusion.126
  357.9 6.7 fusion.83
  384.3 15.1 %collective-permute-done.2 = bf16[768,2,384]{0,2,1:T(8,128)(2,1)} collective-permute-done((bf16[768,2,384]{0,2,1:T(8,128)(2,1)}, bf16[768,2,384]{0,2,1:T(8,128)(2,1)}, u32[]{:S(2)}, u32[]{:S(2)}) %collective-permute-start.2) | collective-permute-done | bytes 1179680 | tf_op jit(solution)/shard_map/ppermute | solution.py:33
  399.4 7.9 collective-permute-done.3
  419.4 5.2 copy.169
  424.6 4.6 all-to-all-start.1
  433.4 111.0 %psum.15 = f32[2,128]{1,0:T(2,128)} all-reduce(f32[2,128]{1,0:T(2,128)S(1)} %pad_maximum_fusion.3), channel_id=1, replica_groups=mesh['tm'=32,'head'=4,'dp'=2] {'tm','head','dp'}, use_global_device_ids=true, to_apply=%region_14.15 | all-reduce | flops 256 | bytes 2048 | tf_op jit(solution)/shard_map/psum | solution.py:154
  547.8 434.3 %all-reduce.2.cloned.1.call-done = f32[384,3072]{1,0:T(8,128)} async-done(((f32[384,3072]{1,0:T(8,128)}), f32[384,3072]{1,0:T(8,128)}) %all-reduce.2.cloned.1.call-update) | async-done | bytes 4718608 | tf_op jit(solution)/shard_map/psum | solution.py:163
  (172 shorter events, 127.0 us)
Async XLA Ops:
  12.7 3.9 copy-start.25
  12.7 42.2 %all-to-all-start = ((bf16[1,192,3,1536]{1,2,0,3:T(4,128)(2,1)}), bf16[1,192,3,1536]{1,2,0,3:T(4,128)(2,1)S(1)}, u32[]{:S(2)}, u32[]{:S(2)}) async-start(bf16[1,192,3,1536]{1,2,0,3:T(4,128)(2,1)} %copy.141), calls=%async_computation | async-start | bytes 6291456 | tf_op jit(solution)/shard_map/all_to_all | solution.py:71
  16.5 135.7 %all-gather.3.cloned.1.call-start = ((), (), s32[]{:S(2)}) async-start(), calls=%async_computation.3 | async-start | bytes 3538944 | tf_op jit(solution)/shard_map/all_gather | solution.py:103
  17.2 65.7 %copy-start.22 = (f32[128]{0:T(128)}, f32[128]{0:T(128)S(1)}, u32[]{:S(2)}) copy-start(f32[128]{0:T(128)S(1)} %get-tuple-element.348) | copy-start | bytes 1540
  62.8 20.1 %copy-start.2 = (bf16[768,3,3,128]{3,2,0,1:T(4,128)(2,1)}, bf16[768,3,3,128]{3,2,0,1:T(4,128)(2,1)S(1)}, u32[]{:S(2)}) copy-start(bf16[768,3,3,128]{3,2,0,1:T(4,128)(2,1)S(1)} %reshape_squeeze.10) | copy-start | bytes 5308420
  64.4 6.6 copy-start
  66.8 7.9 copy-start.15
  67.0 7.7 copy-start.19
  74.7 29.7 %collective-permute-start = (bf16[768,2,384]{0,2,1:T(8,128)(2,1)}, bf16[768,2,384]{0,2,1:T(8,128)(2,1)}, u32[]{:S(2)}, u32[]{:S(2)}) collective-permute-start(bf16[768,2,384]{0,2,1:T(8,128)(2,1)} %pad_maximum_fusion.2), channel_id=1, source_target_pairs={{0,8},{8,16},{16,24},{24,32},{32,40},{40,48},{48,56},{56,64},{64,7... | collective-permute-start | bytes 3538952 | tf_op jit(solution)/shard_map/ppermute | solution.py:21
  78.6 29.6 %collective-permute-start.1 = (bf16[768,2,384]{0,2,1:T(8,128)(2,1)}, bf16[768,2,384]{0,2,1:T(8,128)(2,1)}, u32[]{:S(2)}, u32[]{:S(2)}) collective-permute-start(bf16[768,2,384]{0,2,1:T(8,128)(2,1)} %pad_maximum_fusion.2), channel_id=1, source_target_pairs={{8,0},{16,8},{24,16},{32,24},{40,32},{48,40},{56,48},{64,56},{72,6... | collective-permute-start | bytes 3538952 | tf_op jit(solution)/shard_map/ppermute | solution.py:23
  81.7 137.8 %reduce-scatter.2.cloned.1.call-start = ((), (), s32[]{:S(2)}) async-start(), calls=%async_computation.4 | async-start | bytes 5898240 | tf_op jit(solution)/shard_map/reduce_scatter | solution.py:104
  82.8 25.4 %copy-start.12 = (bf16[768,1,3,128]{0,3,2,1:T(8,128)(2,1)S(1)}, bf16[768,1,3,128]{0,3,2,1:T(8,128)(2,1)}, u32[]{:S(2)}) copy-start(bf16[768,1,3,128]{0,3,2,1:T(8,128)(2,1)} %copy.148) | copy-start | bytes 1769476
  82.9 21.6 %copy-start.10 = (f32[768,3]{1,0:T(8,128)}, f32[768,3]{1,0:T(8,128)S(1)}, u32[]{:S(2)}) copy-start(f32[768,3]{1,0:T(8,128)S(1)} %add_rsqrt_fusion) | copy-start | bytes 27652
  114.2 2.2 copy-start.21
  152.2 7.3 copy-start.7
  159.5 59.9 %copy-start.18 = (bf16[1,192,3072]{2,1,0:T(8,128)(2,1)S(1)}, bf16[1,192,3072]{2,1,0:T(8,128)(2,1)}, u32[]{:S(2)}) copy-start(bf16[1,192,3072]{2,1,0:T(8,128)(2,1)} %param.16) | copy-start | bytes 3538948
  159.6 106.3 %all-gather.5.cloned.1.call-start = ((), (), s32[]{:S(2)}) async-start(), calls=%async_computation.5 | async-start | bytes 5898240 | tf_op jit(solution)/shard_map/all_gather | solution.py:119
  222.2 759.8 %all-reduce.2.cloned.1.call-start = ((), (), s32[]{:S(2)}) async-start(), calls=%async_computation.6 | async-start | bytes 9437184 | tf_op jit(solution)/shard_map/psum | solution.py:163
  298.1 3.9 copy-start.5
  311.0 1.8 copy-start.4
  326.1 3.9 copy-start.5
  338.9 1.8 copy-start.4
  354.1 3.9 copy-start.5
  367.2 7.9 copy-start.6
  368.9 30.5 %collective-permute-start.2 = (bf16[768,2,384]{0,2,1:T(8,128)(2,1)}, bf16[768,2,384]{0,2,1:T(8,128)(2,1)}, u32[]{:S(2)}, u32[]{:S(2)}) collective-permute-start(bf16[768,2,384]{0,2,1:T(8,128)(2,1)} %bitcast.46), channel_id=1, source_target_pairs={{8,0},{16,8},{24,16},{32,24},{40,32},{48,40},{56,48},{64,56},{72,6... | collective-permute-start | bytes 3538952 | tf_op jit(solution)/shard_map/ppermute | solution.py:33
  371.4 35.8 %collective-permute-start.3 = (bf16[768,2,384]{0,2,1:T(8,128)(2,1)}, bf16[768,2,384]{0,2,1:T(8,128)(2,1)}, u32[]{:S(2)}, u32[]{:S(2)}) collective-permute-start(bf16[768,2,384]{0,2,1:T(8,128)(2,1)} %bitcast.47), channel_id=1, source_target_pairs={{0,8},{8,16},{16,24},{24,32},{32,40},{40,48},{48,56},{56,64},{64,7... | collective-permute-start | bytes 3538952 | tf_op jit(solution)/shard_map/ppermute | solution.py:33
  375.7 2.1 copy-start.9
  375.7 2.2 copy-start.11
  375.8 2.2 copy-start.23
  413.8 4.1 copy-start.17
  424.6 4.6 copy-start.16
  424.6 119.9 %all-to-all-start.1 = ((bf16[1,768,3,384]{3,2,0,1:T(4,128)(2,1)}), bf16[1,768,3,384]{3,2,0,1:T(4,128)(2,1)}, u32[]{:S(2)}, u32[]{:S(2)}) async-start(bf16[1,768,3,384]{3,2,0,1:T(4,128)(2,1)} %copy.169), calls=%async_computation.2 | async-start | bytes 4718592 | tf_op jit(solution)/shard_map/all_to_all | solution.py:160
  (11 other events, 14.8 us)
Sparse Core Ops, SparseCore 0:
  81.8 41.4 all-gather.2
  159.7 59.6 reduce-scatter.1
  222.4 43.4 all-gather.4
  364.7 617.2 all-reduce.1
where the time goes:
time: 999 us; the launch traced here: 992 us
  waiting for transfers between devices  621 us (62%)
  blocking collectives  111 us (11%)
  local copies, waits for them, and re-layouts  102 us (10%)
  matrix products  74 us (7%)
  other arithmetic  47.8 us (5%)
  starting transfers between devices  22.1 us (2%)
  between operations  14.2 us (1%)
    psum x1, waiting for transfers between devices, per_device(): everything = lax.psum(grad_proj_local, ('tm', 'dp'))  434 us
    psum x1, blocking collectives, per_device(): lax.psum(jnp.stack([gain_query, gain_key], axis=0), ('tm', 'head', 'dp'))  111 us
    reduce_scatter x1, waiting for transfers between devices, per_device(): lax.psum_scatter(jnp.dot(attn_rows, proj_local, preferred_element_type=jn...  59 us
    dot_general x14, matrix products, contract(): lax.dot_general(left_arr, right_arr, (((left_dim,), (right_dim,)), ((), (...  53.6 us
    all_gather x1, waiting for transfers between devices, per_device(): grad_slab = lax.all_gather(grad_rows, 'head', axis=0, tiled=True)  43.4 us
    all_to_all x1, waiting for transfers between devices, per_device(): lax.all_to_all(qkv, 'head', split_axis=3, concat_axis=1, tiled=True)  37.8 us
    dynamic_update_slice x3, local copies, waits for them, and re-layouts, per_device(): lax.map(backprop, (query_heads, key_heads, value_heads, chances, grad_hea...  33.4 us
    ppermute x2, waiting for transfers between devices, shifted(): return lax.ppermute(array, axis, pairs)  23 us
  transfers between devices with their start and end apart: 10, of which 8 were waited for; matrix products, arithmetic and copies ran while one was open for 8% of the time, Pallas kernels for 0%

commit v1 on v0

v1 whole, which is shorter than its diff:
```python
import math

import jax
import jax.numpy as jnp
from jax import lax
from jax.experimental import pallas as pl
from jax.experimental.pallas import tpu as pltpu
from jax.sharding import PartitionSpec as P

TILE = 384
EPSILON = 1e-06
LOG2_DECAY = math.log2(0.99)
HD = 128
NH = 3
GROUPS = 4
TOK = 192
SLAB = 768
D = 3072
DC = 768
NZ = 8
NY = 4
SCORE_SCALE = HD ** (-0.5)
LOG2E = 1.4426950408889634
BF = jnp.bfloat16
F32 = jnp.float32
MESH = pl.DeviceIdType.MESH


def dot(a, b, da, db):
    return lax.dot_general(a, b, (((da,), (db,)), ((), ())), preferred_element_type=F32)


def unit_of(raw):
    inverse = lax.rsqrt(jnp.mean(raw * raw, axis=-1, keepdims=True) + EPSILON)
    return raw * inverse, inverse


class Links:
    def __init__(self, send, recv, local):
        self.send, self.recv, self.local = send, recv, local
        self.n_remote = self.n_local = 0
        self.open = []

    def put(self, src, dst, device):
        i = self.n_remote
        self.n_remote += 1
        copy = pltpu.make_async_remote_copy(
            src_ref=src,
            dst_ref=dst,
            send_sem=self.send.at[i],
            recv_sem=self.recv.at[i],
            device_id=device,
            device_id_type=MESH,
        )
        copy.start()
        self.open.append(copy)
        return copy

    def keep(self, src, dst):
        i = self.n_local
        self.n_local += 1
        copy = pltpu.make_async_copy(src, dst, self.local.at[i])
        copy.start()
        return copy

    def finish(self):
        for copy in self.open:
            copy.wait_send()


N_REMOTE = 180
N_LOCAL = 16


def arrived(copies):
    for copy in copies:
        copy.wait_recv()


def mega(
    windows, qkv, wsh, tgt, ids, ema_value, ema_steps, gains,
    grad_out, gp_out, gains_out,
    tw, xin, dx, kvq, halo, pt, inv, attg, wbuf, tbuf, twb, gout,
    gas, gar, gao, gax, gxr, gkeep,
    gp, r1, passing, gp2, rl, gp3, r4, fin,
    hsend, hgrad, dkv, dout, dsb,
    gpart, gx, gz, gy,
    send, recv, local,
):
    links = Links(send, recv, local)
    tm = lax.axis_index("tm")
    head = lax.axis_index("head")
    dp = lax.axis_index("dp")
    y, z = tm // NZ, lax.rem(tm, NZ)
    xh, core = head // 2, lax.rem(head, 2)
    line = head * 2 + dp

    def at_line(k):
        b = lax.rem(line + k, 8)
        return {"head": b // 2, "dp": lax.rem(b, 2)}

    def at_z(k):
        return {"tm": y * NZ + lax.rem(z + k, NZ)}

    def at_y(k):
        return {"tm": lax.rem(y + k, NY) * NZ + z}

    right = {"tm": lax.rem(tm + 1, 32)}
    left = {"tm": lax.rem(tm + 31, 32)}
    sib_head = xh * 2 + (1 - core)
    cross_head = (1 - xh) * 2 + core
    diag_head = (1 - xh) * 2 + (1 - core)
    sibling, cross = {"head": sib_head}, {"head": cross_head}
    peers = [cross_head, diag_head, sib_head]

    barrier = pltpu.get_barrier_semaphore()
    greet = [at_line(k) for k in range(1, 8)] + [at_z(k) for k in range(1, 8)]
    greet += [at_y(k) for k in range(1, 4)] + [right, left]
    for device in greet:
        pl.semaphore_signal(barrier, inc=1, device_id=device, device_id_type=MESH)

    def pre(h):
        for j in range(GROUPS):
            c = slice((j * NH + h) * HD, (j * NH + h + 1) * HD)
            xin[j, h, :, :HD] = (unit_of(qkv[1, :, c].astype(F32))[0] * gains[1:2]).astype(BF)
            xin[j, h, :, HD : 2 * HD] = qkv[2, :, c]
            xin[j, h, :, 2 * HD :] = (unit_of(qkv[0, :, c].astype(F32))[0] * gains[0:1]).astype(BF)

    pre(0)
    powers = jnp.exp2(ema_steps[...].astype(F32) * LOG2_DECAY)
    stream_weight = (1.0 - powers) / ema_value[...]
    token_weight = jnp.zeros((1, TOK), F32)
    for i in range(ema_value.shape[1]):
        token_weight = jnp.where(ids[...] == i, stream_weight[:, i : i + 1], token_weight)
    tw[...] = jnp.zeros((8, 256), F32)
    tw[0:1, :TOK] = token_weight
    pl.semaphore_wait(barrier, len(greet))

    my_tok = pl.ds(pl.multiple_of(head * TOK, TOK), TOK)
    my_row = pl.ds(pl.multiple_of(y * 48, 48), 48)

    def tok_of(h):
        return pl.ds(pl.multiple_of(h * TOK, TOK), TOK)

    def send_heads(h):
        out = [links.put(xin.at[p, h], kvq.at[h, my_tok], {"head": p}) for p in peers]
        own = links.keep(xin.at[head, h], kvq.at[h, my_tok])
        return out, own

    def send_halo(h):
        src = kvq.at[h, :, pl.ds(0, 2 * HD)]
        return [links.put(src, halo.at[0, h], right), links.put(src, halo.at[1, h], left)]

    wx = []
    for k in range(1, 8):
        b = lax.rem(line + k, 8)
        cols = pl.ds(pl.multiple_of((b // 2) * DC, DC), DC)
        wx.append(links.put(wsh.at[my_row, cols], wbuf.at[line, my_row], at_line(k)))
    wown = links.keep(
        wsh.at[my_row, pl.ds(pl.multiple_of(head * DC, DC), DC)], wbuf.at[line, my_row]
    )
    x0 = send_heads(0)
    pre(1)
    pre(2)

    ahead = jnp.where(z < NZ // 2, NY - 1, 1)
    back = NY - ahead

    def row_of(k):
        return pl.ds(pl.multiple_of(lax.rem(y + k, NY) * 48, 48), 48)

    def share_w(k, to):
        rows = row_of(k)
        return links.put(wbuf.at[:, rows], wbuf.at[:, rows], at_y(to))

    arrived(wx)
    wown.wait()
    wy = [share_w(0, ahead), share_w(0, back)]
    arrived(x0[0])
    x0[1].wait()
    z0 = send_halo(0)
    x1 = send_heads(1)

    def kv(h, t):
        return kvq.at[h] if t == 1 else halo.at[t // 2, h]

    scale2 = SCORE_SCALE * LOG2E
    query_tile = lax.broadcasted_iota(jnp.int32, (1, SLAB), 1) // TILE

    def reach(h, t):
        if t == 1:
            return jnp.float32(1.0)
        present = tm > 0 if t == 0 else tm < 31
        return jnp.where(present, windows[h, 0].astype(F32), 0.0)

    def scores(h, t):
        ref = kv(h, t)
        q = kvq[h, :, 2 * HD :]
        along, across = reach(h, t), windows[h, 1].astype(F32)

        @pl.loop(0, 2)
        def _(b):
            k = ref[pl.ds(pl.multiple_of(b * TILE, TILE), TILE), :HD]
            s = dot(k, q, 1, 1)
            allowed = along * jnp.where(query_tile == b, 1.0, across)
            p = jnp.exp2(s * scale2 + (allowed - 1.0) * 1e30)
            pt[h, pl.ds(pl.multiple_of((t * 2 + b) * TILE, TILE), TILE), :] = p.astype(BF)

    ones_t = jnp.ones((HD, SLAB), BF)

    def attend(h):
        total = None
        for t in (1, 0, 2):
            vt = jnp.transpose(kv(h, t)[:, HD : 2 * HD])
            part = dot(jnp.concatenate([vt, ones_t], axis=0), pt[h, t * SLAB : (t + 1) * SLAB, :], 1, 0)
            total = part if total is None else total + part
        inverse = 1.0 / total[HD:]
        inv[h] = jnp.transpose(inverse)
        att = jnp.transpose(total[:HD] * inverse).astype(BF)
        attg[:, pl.ds(pl.multiple_of(head * TILE + h * HD, HD), HD)] = att

    scores(0, 1)
    arrived(x1[0])
    x1[1].wait()
    arrived(wy[:1])
    wy[:1] = [share_w(back, ahead)]
    z1 = send_halo(1)
    x2 = send_heads(2)
    scores(1, 1)
    arrived(x2[0])
    x2[1].wait()
    z2 = send_halo(2)
    tx = []
    for p in peers:
        cols = pl.ds(pl.multiple_of(p * DC, DC), DC)
        tx.append(links.put(tgt.at[:, cols], tbuf.at[head], {"head": p}))
        tx.append(links.put(tw, twb.at[head], {"head": p}))
    town = links.keep(tgt.at[:, pl.ds(pl.multiple_of(head * DC, DC), DC)], tbuf.at[head])
    twown = links.keep(tw, twb.at[head])
    scores(2, 1)

    def att_cols(g, h):
        return pl.ds(pl.multiple_of(g * TILE + h * HD, HD), HD)

    att_in, att_fwd = [], []

    def forward(h):
        arrived([att_in[h][0]])
        cols = att_cols(cross_head, h)
        att_fwd.append(links.put(attg.at[:, cols], attg.at[:, cols], sibling))

    for h, zh in enumerate((z0, z1, z2)):
        arrived(zh)
        scores(h, 0)
        scores(h, 2)
        attend(h)
        cols = att_cols(head, h)
        mine = attg.at[:, cols]
        att_in.append([links.put(mine, mine, cross), links.put(mine, mine, sibling)])
        if h > 0:
            forward(h - 1)
    forward(2)
    arrived(wy)
    arrived([c[1] for c in att_in])
    arrived(att_fwd)

    arrived(tx)
    town.wait()
    twown.wait()

    @pl.loop(0, GROUPS)
    def _(i):
        rows = pl.ds(pl.multiple_of(i * TOK, TOK), TOK)
        w = wbuf[...].reshape(GROUPS * TILE, DC)
        out = dot(attg[rows, :], w, 1, 0)
        col = jnp.transpose(jnp.broadcast_to(twb[i, 0:1, :], (HD, 256)))[:TOK, 0:1]
        gout[rows, :] = (col * (out - tbuf[i].astype(F32))).astype(BF)

    def w_rows(group, h):
        w = wbuf[pl.ds(group * 2, 2)].reshape(TILE, DC)
        return w[h * HD : (h + 1) * HD]

    sib_in = []
    for h in range(NH):
        w = jnp.concatenate([w_rows(sib_head, h), w_rows(diag_head, h)], axis=0)
        gas[h] = dot(gout[...], w, 1, 1).astype(BF)
        sib_in.append(links.put(gas.at[h], gar.at[h], sibling))
    for h in range(NH):
        w = jnp.concatenate([w_rows(head, h), w_rows(cross_head, h)], axis=0)
        gao[h] = dot(gout[...], w, 1, 1)
    cross_in = []
    for h in range(NH):
        arrived([sib_in[h]])
        total = gao[h] + gar[h].astype(F32)
        gkeep[h] = total[:, :HD]
        gax[h] = total[:, HD:].astype(BF)
        cross_in.append(links.put(gax.at[h], gxr.at[h], cross))

    @pl.loop(0, GROUPS)
    def _(g):
        a = attg[:, pl.ds(pl.multiple_of(g * TILE, TILE), TILE)]
        part = dot(a, gout[...], 0, 0).astype(BF)
        gp[2 * g] = part[:TOK]
        gp[2 * g + 1] = part[TOK:]

    ry_far = links.put(gp.at[:, row_of(2)], r1.at[0], at_y(ahead))
    ry_back = links.put(gp.at[:, row_of(back)], r1.at[1], at_y(back))

    lane = lax.broadcasted_iota(jnp.int32, (SLAB, HD), 1)

    def backward(h):
        arrived([cross_in[h]])
        g = (gkeep[h] + gxr[h].astype(F32)).astype(BF).astype(F32)
        g2 = (g * inv[h]).astype(BF)
        att = attg[:, att_cols(head, h)].astype(F32)
        diagonal = jnp.sum(g2.astype(F32) * att, axis=1, keepdims=True)
        high = diagonal.astype(BF).astype(F32)
        low = diagonal - high
        extra = jnp.where(lane == 0, -high, jnp.where(lane == 1, -low, 0.0)).astype(BF)
        gext = jnp.concatenate([g2, extra], axis=1)
        q = kvq[h, :, 2 * HD :]
        sent = []
        dq = None
        for t in (0, 2, 1):
            ref = kv(h, t)
            for b in range(2):
                rows = pl.ds(b * TILE, TILE)
                v = jnp.concatenate([ref[rows, HD : 2 * HD], jnp.ones((TILE, HD), BF)], axis=1)
                d = dot(v, gext, 1, 1)
                p = pt[h, (t * 2 + b) * TILE : (t * 2 + b + 1) * TILE, :]
                ds = (p.astype(F32) * d).astype(BF)
                dsb[rows, :] = ds
                dv = dot(p, g2, 1, 0)
                dk = dot(ds, q, 1, 0) * SCORE_SCALE
                if t == 1:
                    dkv[h, rows, :HD] = dk
                    dkv[h, rows, HD:] = dv
                else:
                    hsend[t // 2, h, rows, :HD] = dk.astype(BF)
                    hsend[t // 2, h, rows, HD:] = dv.astype(BF)
            if t == 0:
                sent.append(links.put(hsend.at[0, h], hgrad.at[1, h], left))
            if t == 2:
                sent.append(links.put(hsend.at[1, h], hgrad.at[0, h], right))
            kt = jnp.transpose(ref[:, :HD])
            part = dot(kt, dsb[...], 1, 0)
            dq = part if dq is None else dq + part
        dq = jnp.transpose(dq) * SCORE_SCALE
        dout[h, :, 2 * HD :] = dq.astype(BF)
        gain = jnp.sum(dq * q.astype(F32), axis=0, keepdims=True)
        q_cols = pl.ds(2 * HD, HD)
        back = [
            links.put(dout.at[h, tok_of(p), q_cols], dx.at[head, h, :, q_cols], {"head": p})
            for p in peers
        ]
        return sent, gain, back

    sent0, gq0, back0 = backward(0)
    arrived([ry_far])
    passing[...] = (gp[:, row_of(ahead)].astype(F32) + r1[0].astype(F32)).astype(BF)
    ry_ahead = links.put(passing, r1.at[2], at_y(ahead))
    sent1, gq1, back1 = backward(1)
    sent2, gq2, back2 = backward(2)

    def chunk(zz):
        return gp3.at[zz // 2, :, pl.ds(pl.multiple_of(lax.rem(zz, 2) * TILE, TILE), TILE)]

    def fold(h, sent):
        arrived(sent)
        total = dkv[h] + hgrad[0, h].astype(F32) + hgrad[1, h].astype(F32)
        dout[h, :, : 2 * HD] = total.astype(BF)
        gain = jnp.sum(total[:, :HD] * kvq[h, :, :HD].astype(F32), axis=0, keepdims=True)
        kv_cols = pl.ds(0, 2 * HD)
        back = [
            links.put(dout.at[h, tok_of(p), kv_cols], dx.at[head, h, :, kv_cols], {"head": p})
            for p in peers
        ]
        own = links.keep(dout.at[h, my_tok], dx.at[head, h])
        return gain, back, own

    def post(h):
        cols = []
        for j in range(GROUPS):
            c = slice((j * NH + h) * HD, (j * NH + h + 1) * HD)
            for i, o in ((0, 2), (1, 0)):
                unit, inverse = unit_of(qkv[i, :, c].astype(F32))
                e = dx[j, h, :, o * HD : (o + 1) * HD].astype(F32) * gains[i : i + 1]
                mean = jnp.mean(e * unit, axis=-1, keepdims=True)
                grad_out[i, :, c] = (inverse * (e - unit * mean)).astype(BF)
            grad_out[2, :, c] = dx[j, h, :, HD : 2 * HD]

    gk0, fold0, own0 = fold(0, sent0)
    arrived([ry_back, ry_ahead])
    gp2[...] = (gp[:, my_row].astype(F32) + r1[1].astype(F32) + r1[2].astype(F32)).astype(BF)
    rline = [
        links.put(gp2.at[lax.rem(line + k, 8)], rl.at[line], at_line(k)) for k in range(1, 8)
    ]
    rown = links.keep(gp2.at[line], rl.at[line])
    gk1, fold1, own1 = fold(1, sent1)
    gk2, fold2, own2 = fold(2, sent2)
    arrived(rline)
    rown.wait()
    for j in range(GROUPS):
        gp3[j] = (rl[2 * j].astype(F32) + rl[2 * j + 1].astype(F32)).astype(BF)
    rz = [links.put(chunk(lax.rem(z + k, NZ)), r4.at[k - 1], at_z(k)) for k in range(1, 8)]

    part = jnp.concatenate(
        [gq0 + gq1 + gq2, gk0 + gk1 + gk2, jnp.zeros((6, HD), F32)], axis=0
    )
    gpart[0] = part
    gains_x = [links.put(gpart.at[0], gx.at[k - 1], at_line(k)) for k in range(1, 8)]
    arrived(back0)
    arrived(fold0)
    own0.wait()
    post(0)
    arrived(gains_x)
    for k in range(7):
        part = part + gx[k]
    gpart[1] = part
    gains_z = [links.put(gpart.at[1], gz.at[k - 1], at_z(k)) for k in range(1, 8)]

    arrived(rz)
    total = chunk(z)[...].astype(F32)
    for k in range(7):
        total = total + r4[k].astype(F32)
    fin[...] = total.astype(BF)

    def place(zz):
        cols = pl.ds(pl.multiple_of(zz * TILE, TILE), TILE)
        return gp_out.at[my_row, cols]

    az = [links.put(fin, place(z), at_z(k)) for k in range(1, 8)]
    ay = [links.put(fin, place(z), at_y(k)) for k in range(1, 4)]
    azown = links.keep(fin, place(z))
    arrived(gains_z)
    for k in range(7):
        part = part + gz[k]
    gpart[2] = part
    gains_y = [links.put(gpart.at[2], gy.at[k - 1], at_y(k)) for k in range(1, 4)]
    arrived(back1)
    arrived(fold1)
    own1.wait()
    post(1)
    for i in (0, 6, 1, 5, 2, 4, 3):
        arrived([az[i]])
        got = place(lax.rem(z + NZ - 1 - i, NZ))
        ay += [links.put(got, got, at_y(k)) for k in range(1, 4)]
    arrived(gains_y)
    for k in range(3):
        part = part + gy[k]
    gains_out[...] = part[:2] / gains[...]
    arrived(back2)
    arrived(fold2)
    own2.wait()
    post(2)
    azown.wait()
    arrived(ay)
    links.finish()


def run_mega(*operands):
    any_spec = pl.BlockSpec(memory_space=pl.ANY)
    vmem = pl.BlockSpec(memory_space=pltpu.VMEM)
    v = pltpu.VMEM
    scratch = [
        v((8, 256), F32),
        v((GROUPS, NH, TOK, 3 * HD), BF),
        v((GROUPS, NH, TOK, 3 * HD), BF),
        v((NH, SLAB, 3 * HD), BF),
        v((2, NH, SLAB, 2 * HD), BF),
        v((NH, 3 * SLAB, SLAB), BF),
        v((NH, SLAB, HD), F32),
        v((SLAB, GROUPS * TILE), BF),
        v((8, TOK, DC), BF),
        v((GROUPS, TOK, DC), BF),
        v((GROUPS, 8, 256), F32),
        v((SLAB, DC), BF),
        v((NH, SLAB, 2 * HD), BF),
        v((NH, SLAB, 2 * HD), BF),
        v((NH, SLAB, 2 * HD), F32),
        v((NH, SLAB, HD), BF),
        v((NH, SLAB, HD), BF),
        v((NH, SLAB, HD), F32),
        v((8, TOK, DC), BF),
        v((3, 8, 48, DC), BF),
        v((8, 48, DC), BF),
        v((8, 48, DC), BF),
        v((8, 48, DC), BF),
        v((GROUPS, 48, DC), BF),
        v((7, 48, TILE), BF),
        v((48, TILE), BF),
        v((2, NH, SLAB, 2 * HD), BF),
        v((2, NH, SLAB, 2 * HD), BF),
        v((NH, SLAB, 2 * HD), F32),
        v((NH, SLAB, 3 * HD), BF),
        v((SLAB, SLAB), BF),
        v((3, 8, HD), F32),
        v((7, 8, HD), F32),
        v((7, 8, HD), F32),
        v((3, 8, HD), F32),
        pltpu.SemaphoreType.DMA((N_REMOTE,)),
        pltpu.SemaphoreType.DMA((N_REMOTE,)),
        pltpu.SemaphoreType.DMA((N_LOCAL,)),
    ]
    return pl.pallas_call(
        mega,
        out_shape=(
            jax.ShapeDtypeStruct((3, TOK, GROUPS * TILE), BF),
            jax.ShapeDtypeStruct((TOK, D), BF),
            jax.ShapeDtypeStruct((2, HD), F32),
        ),
        in_specs=[pl.BlockSpec(memory_space=pltpu.SMEM), vmem, any_spec, any_spec] + [vmem] * 4,
        out_specs=(vmem, vmem, vmem),
        scratch_shapes=scratch,
        compiler_params=pltpu.CompilerParams(
            collective_id=1, has_side_effects=True, vmem_limit_bytes=62 * 2**20
        ),
        name="mega",
    )(*operands)


def per_device(qkv, norm_gains, windows, proj_weight, target, stream_ids, ema_value, ema_steps):
    grad_qkv, gp, grad_gains = run_mega(
        windows,
        qkv[0].transpose(1, 0, 2),
        proj_weight,
        target[0],
        stream_ids,
        ema_value[None],
        ema_steps[None],
        norm_gains,
    )
    return (grad_qkv.transpose(1, 0, 2)[None], gp.astype(F32), grad_gains)


def solution(mesh):
    return jax.shard_map(
        per_device,
        mesh=mesh,
        in_specs=(
            P("dp", ("tm", "head"), None, None),
            P(),
            P("head", None),
            P(("head", "dp"), None),
            P("dp", ("tm", "head"), None),
            P("dp", ("tm", "head")),
            P(),
            P(),
        ),
        out_specs=(P("dp", ("tm", "head"), None, None), P(("head", "dp"), None), P()),
        check_vma=False,
    )
```

time: 999 us -> 175 us (0.18)
  waiting for transfers between devices: 621 us -> 0 us
  Pallas kernels: 0 us -> 165 us
  blocking collectives: 111 us -> 0 us
  local copies, waits for them, and re-layouts: 102 us -> 3.11 us
  matrix products: 74 us -> 0 us
  other arithmetic: 47.8 us -> 3.07 us
  starting transfers between devices: 22.1 us -> 0 us
  between operations: 14.2 us -> 0.65 us
    psum x1 -> x0, waiting for transfers between devices: 434 us -> none  [per_device(): everything = lax.psum(grad_proj_local, ('tm', 'dp'))]
    pallas_call x0 -> x1, Pallas kernels: none -> 165 us  [run_mega(): pl.pallas_call(mega, out_shape=(jax.ShapeDtypeStruct((3, TOK, GROUPS * TI...]
    psum x1 -> x0, blocking collectives: 111 us -> none  [per_device(): lax.psum(jnp.stack([gain_query, gain_key], axis=0), ('tm', 'head', 'dp'))]
    dot_general x22 -> x0, matrix products: 74 us -> none  [the longest x14 53.6 us: contract(): lax.dot_general(left_arr, right_arr, (((left_dim,), (right_dim,)), ((), (...]
    reduce_scatter x1 -> x0, waiting for transfers between devices: 59 us -> none  [per_device(): lax.psum_scatter(jnp.dot(attn_rows, proj_local, preferred_element_type=jn...]
    ppermute x4 -> x0, waiting for transfers between devices: 46.3 us -> none  [the longest x2 23 us: shifted(): return lax.ppermute(array, axis, pairs)]
    all_gather x2 -> x0, waiting for transfers between devices: 43.4 us -> none  [the longest x1 43.4 us: per_device(): grad_slab = lax.all_gather(grad_rows, 'head', axis=0, tiled=True)]
    all_to_all x2 -> x0, waiting for transfers between devices: 37.8 us -> none  [the longest x1 37.8 us: per_device(): lax.all_to_all(qkv, 'head', split_axis=3, concat_axis=1, tiled=True)]
  transfers between devices with their start and end apart: 10 -> 0, of which waited for: 8 -> 0; matrix products, arithmetic and copies ran while one was open for 8% -> 0% of each run, Pallas kernels for 0% -> 0%
where the time goes in v1:
time: 175 us; the launch traced here: 172 us
  Pallas kernels  165 us (94%)
  local copies, waits for them, and re-layouts  3.11 us (2%)
  other arithmetic  3.07 us (2%)
    pallas_call x1, Pallas kernels, run_mega(): pl.pallas_call(mega, out_shape=(jax.ShapeDtypeStruct((3, TOK, GROUPS * TI...  165 us

profile of v1, /device:TPU:34, one launch (start us, length us, event | category | flops | bytes accessed | tf_op | source)
XLA Modules:
  0.0 172.2 jit_solution(7721087247387179369)
XLA Ops:
  0.6 1.3 copy.11.windows
  2.0 165.4 %mega.1 = (bf16[3,192,1536]{2,1,0:T(8,128)(2,1)}, bf16[192,3072]{1,0:T(8,128)(2,1)}, f32[2,128]{1,0:T(2,128)}) custom-call(s32[3,2]{1,0:T(4,128)} %copy.11.windows, bf16[3,192,1536]{2,1,0:T(8,128)(2,1)} %bitcast.10, bf16[192,3072]{1,0:T(8,128)(2,1)} %wsh.1, bf16[192,3072]{1,0:T(8,128)(2,1)} %bitcast.11, s32[1,192]{1,0:T(1,128)} %ids.1, f32[1,4]{1,0:T(1,128)} %bitcast.12, ...), custom_call_target="tpu_custom_call" | custom-call | tf_op jit(solution)/shard_map/mega/pallas_call | solution.py:505
  167.4 0.0 copy-start
  167.4 3.1 %convert_element_type.3 = f32[192,3072]{1,0:T(8,128)} convert(bf16[192,3072]{1,0:T(8,128)(2,1)} %get-tuple-element.7) | non-fusion elementwise | flops 589824 | bytes 3538944 | tf_op jit(solution)/shard_map/convert_element_type | solution.py:533
  170.4 0.0 copy-done
  170.4 0.0 copy-start.1
  170.4 1.2 copy.14
  171.6 0.0 copy-done.1
  171.6 0.6 copy.15
Async XLA Ops:
  167.4 3.1 %copy-start = (bf16[3,192,1536]{2,1,0:T(8,128)(2,1)S(1)}, bf16[3,192,1536]{2,1,0:T(8,128)(2,1)}, u32[]{:S(2)}) copy-start(bf16[3,192,1536]{2,1,0:T(8,128)(2,1)} %get-tuple-element.6) | copy-start | bytes 5308420
  170.4 1.2 copy-start.1

commit v2 on v1

--- a/solution.py
+++ b/solution.py
@@ -151,14 +151,18 @@
         src = kvq.at[h, :, pl.ds(0, 2 * HD)]
         return [links.put(src, halo.at[0, h], right), links.put(src, halo.at[1, h], left)]
 
+    half = lax.rem(z, 2) * TILE
+    my_half = pl.ds(pl.multiple_of(half, TILE), TILE)
+
+    def w_cols(h):
+        return pl.ds(pl.multiple_of(h * DC + half, TILE), TILE)
+
     wx = []
     for k in range(1, 8):
         b = lax.rem(line + k, 8)
-        cols = pl.ds(pl.multiple_of((b // 2) * DC, DC), DC)
-        wx.append(links.put(wsh.at[my_row, cols], wbuf.at[line, my_row], at_line(k)))
-    wown = links.keep(
-        wsh.at[my_row, pl.ds(pl.multiple_of(head * DC, DC), DC)], wbuf.at[line, my_row]
-    )
+        src = wsh.at[my_row, w_cols(b // 2)]
+        wx.append(links.put(src, wbuf.at[line, my_row, my_half], at_line(k)))
+    wown = links.keep(wsh.at[my_row, w_cols(head)], wbuf.at[line, my_row, my_half])
     x0 = send_heads(0)
     pre(1)
     pre(2)
@@ -175,11 +179,15 @@
 
     arrived(wx)
     wown.wait()
-    wy = [share_w(0, ahead), share_w(0, back)]
+    mine = wbuf.at[:, my_row, my_half]
+    wz = links.put(mine, mine, {"tm": tm + 1 - 2 * lax.rem(z, 2)})
+    x1 = send_heads(1)
     arrived(x0[0])
     x0[1].wait()
     z0 = send_halo(0)
-    x1 = send_heads(1)
+    x2 = send_heads(2)
+    arrived([wz])
+    wy = [share_w(0, ahead), share_w(0, back)]
 
     def kv(h, t):
         return kvq.at[h] if t == 1 else halo.at[t // 2, h]
@@ -191,12 +199,12 @@
         if t == 1:
             return jnp.float32(1.0)
         present = tm > 0 if t == 0 else tm < 31
-        return jnp.where(present, windows[h, 0].astype(F32), 0.0)
+        return jnp.where(present, windows[0, h].astype(F32), 0.0)
 
     def scores(h, t):
         ref = kv(h, t)
         q = kvq[h, :, 2 * HD :]
-        along, across = reach(h, t), windows[h, 1].astype(F32)
+        along, across = reach(h, t), windows[1, h].astype(F32)
 
         @pl.loop(0, 2)
         def _(b):
@@ -222,14 +230,7 @@
     scores(0, 1)
     arrived(x1[0])
     x1[1].wait()
-    arrived(wy[:1])
-    wy[:1] = [share_w(back, ahead)]
     z1 = send_halo(1)
-    x2 = send_heads(2)
-    scores(1, 1)
-    arrived(x2[0])
-    x2[1].wait()
-    z2 = send_halo(2)
     tx = []
     for p in peers:
         cols = pl.ds(pl.multiple_of(p * DC, DC), DC)
@@ -237,6 +238,12 @@
         tx.append(links.put(tw, twb.at[head], {"head": p}))
     town = links.keep(tgt.at[:, pl.ds(pl.multiple_of(head * DC, DC), DC)], tbuf.at[head])
     twown = links.keep(tw, twb.at[head])
+    scores(1, 1)
+    arrived(x2[0])
+    x2[1].wait()
+    z2 = send_halo(2)
+    arrived(wy[:1])
+    wy[:1] = [share_w(back, ahead)]
     scores(2, 1)
 
     def att_cols(g, h):
@@ -275,6 +282,16 @@
         out = dot(attg[rows, :], w, 1, 0)
         col = jnp.transpose(jnp.broadcast_to(twb[i, 0:1, :], (HD, 256)))[:TOK, 0:1]
         gout[rows, :] = (col * (out - tbuf[i].astype(F32))).astype(BF)
+
+    @pl.loop(0, GROUPS)
+    def _(g):
+        a = attg[:, pl.ds(pl.multiple_of(g * TILE, TILE), TILE)]
+        part = dot(a, gout[...], 0, 0).astype(BF)
+        gp[2 * g] = part[:TOK]
+        gp[2 * g + 1] = part[TOK:]
+
+    ry_far = links.put(gp.at[:, row_of(2)], r1.at[0], at_y(ahead))
+    ry_back = links.put(gp.at[:, row_of(back)], r1.at[1], at_y(back))
 
     def w_rows(group, h):
         w = wbuf[pl.ds(group * 2, 2)].reshape(TILE, DC)
@@ -295,16 +312,6 @@
         gkeep[h] = total[:, :HD]
         gax[h] = total[:, HD:].astype(BF)
         cross_in.append(links.put(gax.at[h], gxr.at[h], cross))
-
-    @pl.loop(0, GROUPS)
-    def _(g):
-        a = attg[:, pl.ds(pl.multiple_of(g * TILE, TILE), TILE)]
-        part = dot(a, gout[...], 0, 0).astype(BF)
-        gp[2 * g] = part[:TOK]
-        gp[2 * g + 1] = part[TOK:]
-
-    ry_far = links.put(gp.at[:, row_of(2)], r1.at[0], at_y(ahead))
-    ry_back = links.put(gp.at[:, row_of(back)], r1.at[1], at_y(back))
 
     lane = lax.broadcasted_iota(jnp.int32, (SLAB, HD), 1)
 
@@ -356,10 +363,10 @@
         return sent, gain, back
 
     sent0, gq0, back0 = backward(0)
+    sent1, gq1, back1 = backward(1)
     arrived([ry_far])
     passing[...] = (gp[:, row_of(ahead)].astype(F32) + r1[0].astype(F32)).astype(BF)
     ry_ahead = links.put(passing, r1.at[2], at_y(ahead))
-    sent1, gq1, back1 = backward(1)
     sent2, gq2, back2 = backward(2)
 
     def chunk(zz):
@@ -397,12 +404,13 @@
     ]
     rown = links.keep(gp2.at[line], rl.at[line])
     gk1, fold1, own1 = fold(1, sent1)
-    gk2, fold2, own2 = fold(2, sent2)
     arrived(rline)
     rown.wait()
     for j in range(GROUPS):
         gp3[j] = (rl[2 * j].astype(F32) + rl[2 * j + 1].astype(F32)).astype(BF)
     rz = [links.put(chunk(lax.rem(z + k, NZ)), r4.at[k - 1], at_z(k)) for k in range(1, 8)]
+
+    gk2, fold2, own2 = fold(2, sent2)
 
     part = jnp.concatenate(
         [gq0 + gq1 + gq2, gk0 + gk1 + gk2, jnp.zeros((6, HD), F32)], axis=0
@@ -521,7 +529,7 @@
 
 def per_device(qkv, norm_gains, windows, proj_weight, target, stream_ids, ema_value, ema_steps):
     grad_qkv, gp, grad_gains = run_mega(
-        windows,
+        windows.T,
         qkv[0].transpose(1, 0, 2),
         proj_weight,
         target[0],

time: 175 us -> 154 us (0.88); the launches traced: 172 us -> 154 us
  Pallas kernels: 165 us -> 149 us
    pallas_call x1, Pallas kernels: 165 us -> 149 us  [run_mega(): pl.pallas_call(mega, out_shape=(jax.ShapeDtypeStruct((3, TOK, GROUPS * TI...]
where the time goes in v2:
time: 154 us
  Pallas kernels  149 us (97%)
  other arithmetic  3.07 us (2%)
  local copies, waits for them, and re-layouts  1.78 us (1%)
    pallas_call x1, Pallas kernels, run_mega(): pl.pallas_call(mega, out_shape=(jax.ShapeDtypeStruct((3, TOK, GROUPS * TI...  149 us

profile of v2, /device:TPU:34, one launch (start us, length us, event | category | flops | bytes accessed | tf_op | source)
XLA Modules:
  0.0 154.3 jit_solution(15136429492341823319)
XLA Ops:
  0.6 148.8 %mega.1 = (bf16[3,192,1536]{2,1,0:T(8,128)(2,1)}, bf16[192,3072]{1,0:T(8,128)(2,1)}, f32[2,128]{1,0:T(2,128)}) custom-call(s32[2,3]{1,0:T(2,128)} %bitcast.13, bf16[3,192,1536]{2,1,0:T(8,128)(2,1)} %bitcast.10, bf16[192,3072]{1,0:T(8,128)(2,1)} %wsh.1, bf16[192,3072]{1,0:T(8,128)(2,1)} %bitcast.12, s32[1,192]{1,0:T(1,128)} %ids.1, f32[1,4]{1,0:T(1,128)} %bitcast.14, ...), custom_call_target="tpu_custom_call" | custom-call | tf_op jit(solution)/shard_map/mega/pallas_call | solution.py:513
  149.4 0.0 copy-start
  149.4 3.1 %convert_element_type.3 = f32[192,3072]{1,0:T(8,128)} convert(bf16[192,3072]{1,0:T(8,128)(2,1)} %get-tuple-element.7) | non-fusion elementwise | flops 589824 | bytes 3538944 | tf_op jit(solution)/shard_map/convert_element_type | solution.py:541
  152.5 0.0 copy-done
  152.5 0.0 copy-start.1
  152.5 1.2 copy.13
  153.7 0.0 copy-done.1
  153.7 0.6 copy.14
Async XLA Ops:
  149.4 3.1 %copy-start = (bf16[3,192,1536]{2,1,0:T(8,128)(2,1)S(1)}, bf16[3,192,1536]{2,1,0:T(8,128)(2,1)}, u32[]{:S(2)}) copy-start(bf16[3,192,1536]{2,1,0:T(8,128)(2,1)} %get-tuple-element.6) | copy-start | bytes 5308420
  152.5 1.2 copy-start.1
